TPU v7x, 32 devices: a whole 2x2x4 slice. The times are simulated.
32 devices in a mesh: view: 2 (over x), expert: 4 (over z), col: 4 (over y, core).
Axes of the slice: x: 2, y: 2, z: 4, core: 2. Of those that a mesh axis runs over, the one named last changes fastest.
Arguments:
- tokens: bfloat16 [4096, 2560], P(('view', 'expert', 'col')), may hold values from -6 to 6
- expert_ids: int32 [4096, 2], P(('view', 'expert', 'col')), may hold values from 0 to 3, all different within a row; in each aligned block of 128 rows (0 to 127, 128 to 255, ...) at most 68 rows name the same one
- gate_codes: int32 [4096, 2], P(('view', 'expert', 'col')), may hold values from 1 to 1023
- fake_score: bfloat16 [4096, 2560], P(('view', 'expert', 'col')), may hold values from -6 to 6
- gate_weight: bfloat16 [4, 2560, 3456], P('expert', 'view', 'col'), may hold values from -0.125 to 0.125
- up_weight: bfloat16 [4, 2560, 3456], P('expert', 'view', 'col'), may hold values from -0.125 to 0.125
- down_weight: bfloat16 [4, 3456, 2560], P('expert', 'col', 'view'), may hold values from -0.109375 to 0.109375
Outputs:
- score_gap: bfloat16 [4096, 2560], P(('view', 'expert', 'col'))
Inputs may be any that keep to these rules, and one draw needn't show every extreme that they name: `expert_ids`: each row names two different experts; within the 128 rows of one device no expert is named by more than 68 rows, a bound that some block reaches.
All inputs are finite; a program needn't handle non-finite values.
Results may differ from a plain program's by a relative error of at most 0.007.
Values may be sent and summed in bfloat16 or wider, within the bound.
A program may use at most 128 MiB of HBM per device.

v0:
```python
import jax
import jax.numpy as jnp
from jax import lax
from jax.sharding import PartitionSpec as P

D = 2560
NE = 4
CAP = 68


def on_device(tokens, expert_ids, gate_codes, fake_score, gate_weight, up_weight, down_weight):
    slots_all = NE * CAP
    hits = expert_ids[:, :, None] == jnp.arange(NE)[None, None, :]
    routed = jnp.sum(hits.astype(jnp.int32), axis=1)
    before = jnp.cumsum(routed, axis=0) - routed
    slot = jnp.sum(jnp.where(hits, before[:, None, :], 0), axis=2)
    target = expert_ids * CAP + slot
    place = target[:, :, None] == jnp.arange(slots_all)[None, None, :]
    select = jnp.any(place, axis=1).astype(jnp.bfloat16)
    outgoing = jnp.dot(select.T, tokens, preferred_element_type=jnp.float32).astype(jnp.bfloat16)
    arrived = lax.all_to_all(
        outgoing.reshape(NE, CAP, D), "expert", split_axis=0, concat_axis=0, tiled=True
    )
    gathered = lax.all_gather(arrived, "col", axis=0, tiled=True)
    inputs = gathered.reshape(-1, D)

    def add_rows(piece):
        return jnp.dot(inputs, piece[0], preferred_element_type=jnp.float32)

    gate = add_rows(lax.all_gather(gate_weight, "view", axis=1, tiled=True))
    up = add_rows(lax.all_gather(up_weight, "view", axis=1, tiled=True))
    hidden = (jax.nn.silu(gate) * up).astype(jnp.bfloat16)
    partial_out = jnp.dot(
        hidden,
        lax.all_gather(down_weight, "view", axis=2, tiled=True)[0],
        preferred_element_type=jnp.float32,
    ).astype(jnp.bfloat16)
    partial_out = lax.optimization_barrier(partial_out).astype(jnp.float32)
    summed = lax.psum_scatter(
        partial_out.astype(jnp.bfloat16), "col", scatter_dimension=0, tiled=True
    )
    back = lax.all_to_all(
        summed.reshape(NE, CAP, D), "expert", split_axis=0, concat_axis=0, tiled=True
    )
    results = back.reshape(slots_all, D)
    weights = gate_codes.astype(jnp.float32) / 1024.0
    teacher = jnp.zeros((tokens.shape[0], D), jnp.float32)
    for route in range(2):
        picker = place[:, route, :].astype(jnp.bfloat16)
        picked = jnp.dot(picker, results, preferred_element_type=jnp.float32)
        teacher = teacher + weights[:, route][:, None] * picked
    return (fake_score.astype(jnp.float32) - teacher).astype(jnp.bfloat16)


def solution(mesh):
    in_specs = (
        P(("view", "expert", "col"), None),
        P(("view", "expert", "col"), None),
        P(("view", "expert", "col"), None),
        P(("view", "expert", "col"), None),
        P("expert", "view", "col"),
        P("expert", "view", "col"),
        P("expert", "col", "view"),
    )
    out_specs = P(("view", "expert", "col"), None)
    return jax.shard_map(
        on_device, mesh=mesh, in_specs=in_specs, out_specs=out_specs, check_vma=False
    )
```

profile of v0, /device:TPU:0, one launch (start us, length us, event | category | flops | bytes accessed | tf_op | source)
XLA Modules:
  0.0 394.0 jit_solution(5192639153908407928)
XLA Ops:
  6.5 0.0 copy-start
  6.5 0.0 all-gather.5.cloned.1.call-start
  6.5 0.8 convert_reduce_fusion
  7.3 0.1 copy.12
  7.4 0.2 reduce_window_sum.11
  7.6 0.1 copy.14
  7.7 0.7 select_reduce_fusion
  8.4 0.7 multiply_add_fusion
  9.1 0.7 iota_compare_fusion
  9.8 0.0 copy-done
  9.8 0.5 convolution_convert_fusion.1
  10.3 0.3 reshape.23
  10.6 41.1 %all_to_all.10 = bf16[4,68,2560]{2,1,0:T(8,128)(2,1)} all-to-all(bf16[4,68,2560]{2,1,0:T(8,128)(2,1)S(1)} %reshape.23), channel_id=1, replica_groups=mesh['view'=2,'expert'=4,'col'=4] {'expert'}, dimensions={0} | all-to-all | bytes 2785280 | tf_op jit(solution)/shard_map/all_to_all | solution.py:21
  51.7 0.0 all-gather.5.cloned.1.call-update
  51.7 0.0 all-gather.7.cloned.1.call-start
  51.8 0.7 all-gather.7.cloned.1.call-update
  52.5 0.0 all-gather.9.cloned.1.call-start
  52.5 0.7 all-gather.9.cloned.1.call-update
  53.2 0.0 all-gather.11.cloned.1.call-start
  53.3 0.5 all-gather.11.cloned.1.call-update
  53.8 0.0 reduce-scatter.2.cloned.1.call-start
  53.8 41.3 %all-gather.5.cloned.1.call-done = bf16[16,68,2560]{2,1,0:T(8,128)(2,1)} async-done(((bf16[4,68,2560]{2,1,0:T(8,128)(2,1)}), bf16[16,68,2560]{2,1,0:T(8,128)(2,1)}) %all-gather.5.cloned.1.call-update) | async-done | bytes 5570576 | tf_op jit(solution)/shard_map/all_gather | solution.py:24
  95.2 7.9 %reshape.24 = bf16[1088,2560]{1,0:T(8,128)(2,1)} reshape(bf16[16,68,2560]{2,1,0:T(8,128)(2,1)} %all-gather.5.cloned.1.call-done) | data formatting | bytes 11141120 | tf_op jit(solution)/shard_map/reshape | solution.py:25
  103.1 53.0 %all-gather.7.cloned.1.call-done = bf16[1,2560,864]{1,2,0:T(8,128)(2,1)} async-done(((bf16[1,1280,864]{1,2,0:T(8,128)(2,1)}), bf16[1,2560,864]{1,2,0:T(8,128)(2,1)}) %all-gather.7.cloned.1.call-update) | async-done | bytes 4423696 | tf_op jit(solution)/shard_map/all_gather | solution.py:30
  156.1 10.5 %fusion.2 = f32[1088,864]{1,0:T(8,128)} fusion(bf16[1088,2560]{1,0:T(8,128)(2,1)} %reshape.24, bf16[1,2560,864]{1,2,0:T(8,128)(2,1)} %all-gather.7.cloned.1.call-done), kind=kOutput, calls=%fused_computation.4 | convolution fusion | flops 4812963840 | bytes 13754368 | tf_op jit(solution)/shard_map/dot_general | solution.py:28
  166.6 50.4 %all-gather.9.cloned.1.call-done = bf16[1,2560,864]{1,2,0:T(8,128)(2,1)} async-done(((bf16[1,1280,864]{1,2,0:T(8,128)(2,1)}), bf16[1,2560,864]{1,2,0:T(8,128)(2,1)}) %all-gather.9.cloned.1.call-update) | async-done | bytes 4423696 | tf_op jit(solution)/shard_map/all_gather | solution.py:31
  217.0 9.9 %fusion.7 = bf16[1088,864]{1,0:T(8,128)(2,1)S(1)} fusion(bf16[1088,2560]{1,0:T(8,128)(2,1)} %reshape.24, bf16[1,2560,864]{1,2,0:T(8,128)(2,1)} %all-gather.9.cloned.1.call-done, f32[1088,864]{1,0:T(8,128)} %fusion.2), kind=kOutput, calls=%fused_computation.12 | convolution fusion | flops 4818604032 | bytes 15634432 | tf_op jit(solution)/shard_map/dot_general | solution.py:28
  226.9 50.8 %all-gather.11.cloned.1.call-done = bf16[1,864,2560]{2,1,0:T(8,128)(2,1)} async-done(((bf16[1,864,1280]{2,1,0:T(8,128)(2,1)}), bf16[1,864,2560]{2,1,0:T(8,128)(2,1)}) %all-gather.11.cloned.1.call-update) | async-done | bytes 4423696 | tf_op jit(solution)/shard_map/all_gather | solution.py:35
  277.7 10.0 %convolution_convert_fusion = bf16[1088,2560]{1,0:T(8,128)(2,1)} fusion(bf16[1088,864]{1,0:T(8,128)(2,1)S(1)} %fusion.7, bf16[1,864,2560]{2,1,0:T(8,128)(2,1)} %all-gather.11.cloned.1.call-done), kind=kOutput, calls=%fused_computation | convolution fusion | flops 4815749120 | bytes 11874304 | tf_op jit(solution)/shard_map/dot_general | solution.py:33
  287.7 0.0 reduce-scatter.2.cloned.1.call-update
  287.7 0.0 copy-start.1
  287.8 53.7 %reduce-scatter.2.cloned.1.call-done = bf16[272,2560]{1,0:T(8,128)(2,1)} async-done(((bf16[1088,2560]{1,0:T(8,128)(2,1)}), bf16[272,2560]{1,0:T(8,128)(2,1)}) %reduce-scatter.2.cloned.1.call-update) | async-done | bytes 1392656 | tf_op jit(solution)/shard_map/reduce_scatter | solution.py:39
  341.5 2.4 reshape.25
  343.8 4.6 %all-to-all-start.1 = ((bf16[4,68,2560]{2,1,0:T(8,128)(2,1)}), bf16[4,68,2560]{2,1,0:T(8,128)(2,1)S(1)}, u32[]{:S(2)}, u32[]{:S(2)}) async-start(bf16[4,68,2560]{2,1,0:T(8,128)(2,1)} %reshape.25), calls=%async_computation.2 | async-start | bytes 2949120 | tf_op jit(solution)/shard_map/all_to_all | solution.py:42
  348.4 0.0 copy-done.1
  348.5 34.8 %all-to-all-done.1 = bf16[4,68,2560]{2,1,0:T(8,128)(2,1)S(1)} async-done(((bf16[4,68,2560]{2,1,0:T(8,128)(2,1)}), bf16[4,68,2560]{2,1,0:T(8,128)(2,1)S(1)}, u32[]{:S(2)}, u32[]{:S(2)}) %all-to-all-start.1) | async-done | bytes 1392672 | tf_op jit(solution)/shard_map/all_to_all | solution.py:42
  383.3 0.3 reshape.26
  383.6 1.3 convolution_multiply_fusion.2
  384.9 2.5 fusion.6
  (3 shorter events, 0.0 us)
Async XLA Ops:
  6.5 3.2 copy-start
  6.5 88.6 %all-gather.5.cloned.1.call-start = ((), (), s32[]{:S(2)}) async-start(), calls=%async_computation.3 | async-start | bytes 7372800 | tf_op jit(solution)/shard_map/all_gather | solution.py:24
  51.7 104.3 %all-gather.7.cloned.1.call-start = ((), (), s32[]{:S(2)}) async-start(), calls=%async_computation.4 | async-start | bytes 6635520 | tf_op jit(solution)/shard_map/all_gather | solution.py:30
  52.5 164.5 %all-gather.9.cloned.1.call-start = ((), (), s32[]{:S(2)}) async-start(), calls=%async_computation.5 | async-start | bytes 6635520 | tf_op jit(solution)/shard_map/all_gather | solution.py:31
  53.2 224.5 %all-gather.11.cloned.1.call-start = ((), (), s32[]{:S(2)}) async-start(), calls=%async_computation.6 | async-start | bytes 6635520 | tf_op jit(solution)/shard_map/all_gather | solution.py:35
  53.8 287.7 %reduce-scatter.2.cloned.1.call-start = ((), (), s32[]{:S(2)}) async-start(), calls=%async_computation.7 | async-start | bytes 6963200 | tf_op jit(solution)/shard_map/reduce_scatter | solution.py:39
  287.7 60.7 %copy-start.1 = (s32[128,2]{0,1:T(2,128)S(1)}, s32[128,2]{0,1:T(2,128)}, u32[]{:S(2)}) copy-start(s32[128,2]{0,1:T(2,128)} %param.9) | copy-start | bytes 3076
  343.8 39.5 %all-to-all-start.1 = ((bf16[4,68,2560]{2,1,0:T(8,128)(2,1)}), bf16[4,68,2560]{2,1,0:T(8,128)(2,1)S(1)}, u32[]{:S(2)}, u32[]{:S(2)}) async-start(bf16[4,68,2560]{2,1,0:T(8,128)(2,1)} %reshape.25), calls=%async_computation.2 | async-start | bytes 2949120 | tf_op jit(solution)/shard_map/all_to_all | solution.py:42
Sparse Core Ops, SparseCore 0:
  51.8 43.2 all-gather.4
  96.7 59.3 all-gather.6
  157.6 59.3 all-gather.8
  218.4 59.3 all-gather.10
  287.9 53.5 reduce-scatter.1
where the time goes:
time: 395 us; the launch traced here: 394 us
  waiting for transfers between devices  286 us (72%)
  blocking collectives  41.1 us (10%)
  matrix products  34.8 us (9%)
  between operations  13.2 us (3%)
  local copies, waits for them, and re-layouts  11.1 us (3%)
  starting transfers between devices  4.76 us (1%)
    reduce_scatter x1, waiting for transfers between devices, on_device(): lax.psum_scatter(partial_out.astype(jnp.bfloat16), 'col', scatter_dimensi...  53.7 us
    all_gather x1, waiting for transfers between devices, on_device(): gate = add_rows(lax.all_gather(gate_weight, 'view', axis=1, tiled=True))  53 us
    all_gather x1, waiting for transfers between devices, on_device(): lax.all_gather(down_weight, 'view', axis=2, tiled=True)[0]  50.8 us
    all_gather x1, waiting for transfers between devices, on_device(): up = add_rows(lax.all_gather(up_weight, 'view', axis=1, tiled=True))  50.4 us
    all_gather x1, waiting for transfers between devices, on_device(): gathered = lax.all_gather(arrived, 'col', axis=0, tiled=True)  41.3 us
    all_to_all x1, blocking collectives, on_device(): lax.all_to_all(outgoing.reshape(NE, CAP, D), 'expert', split_axis=0, conc...  41.1 us
    all_to_all x1, waiting for transfers between devices, on_device(): lax.all_to_all(summed.reshape(NE, CAP, D), 'expert', split_axis=0, concat...  34.8 us
    dot_general x2, matrix products, add_rows(): return jnp.dot(inputs, piece[0], preferred_element_type=jnp.float32)  20.4 us
  transfers between devices with their start and end apart: 6, of which 6 were waited for; matrix products, arithmetic and copies ran while one was open for 7% of the time, Pallas kernels for 0%

commit v1 on v0

--- a/solution.py
+++ b/solution.py
@@ -9,6 +9,58 @@
 
 
 def on_device(tokens, expert_ids, gate_codes, fake_score, gate_weight, up_weight, down_weight):
+    slots_all = NE * CAP
+    hits = expert_ids[:, :, None] == jnp.arange(NE)[None, None, :]
+    routed = jnp.sum(hits.astype(jnp.int32), axis=1)
+    before = jnp.cumsum(routed, axis=0) - routed
+    slot = jnp.sum(jnp.where(hits, before[:, None, :], 0), axis=2)
+    target = expert_ids * CAP + slot
+    place = target[:, :, None] == jnp.arange(slots_all)[None, None, :]
+    select = jnp.any(place, axis=1).astype(jnp.bfloat16)
+    outgoing = jnp.dot(select.T, tokens, preferred_element_type=jnp.float32).astype(jnp.bfloat16)
+    v = lax.axis_index("view")
+    half = gate_weight.shape[1]
+    swap = [(0, 1), (1, 0)]
+    other = [lax.ppermute(w[0], "view", swap) for w in (gate_weight, up_weight, down_weight)]
+    arrived = lax.all_to_all(
+        outgoing.reshape(NE, CAP, D), "expert", split_axis=0, concat_axis=0, tiled=True
+    )
+    gathered = lax.all_gather(arrived, "col", axis=0, tiled=True)
+    inputs = gathered.reshape(-1, D)
+    mine = lax.dynamic_slice_in_dim(inputs, v * half, half, axis=1)
+    theirs = lax.dynamic_slice_in_dim(inputs, (1 - v) * half, half, axis=1)
+
+    def project(own, far):
+        return jnp.dot(mine, own, preferred_element_type=jnp.float32) + jnp.dot(
+            theirs, far, preferred_element_type=jnp.float32
+        )
+
+    gate = project(gate_weight[0], other[0])
+    up = project(up_weight[0], other[1])
+    hidden = (jax.nn.silu(gate) * up).astype(jnp.bfloat16)
+    near = jnp.dot(hidden, down_weight[0], preferred_element_type=jnp.float32)
+    far = jnp.dot(hidden, other[2], preferred_element_type=jnp.float32)
+    near, far = near.astype(jnp.bfloat16), far.astype(jnp.bfloat16)
+    partial_out = jnp.concatenate(
+        [jnp.where(v == 0, near, far), jnp.where(v == 0, far, near)], axis=1
+    )
+    summed = lax.psum_scatter(
+        partial_out, "col", scatter_dimension=0, tiled=True
+    )
+    back = lax.all_to_all(
+        summed.reshape(NE, CAP, D), "expert", split_axis=0, concat_axis=0, tiled=True
+    )
+    results = back.reshape(slots_all, D)
+    weights = gate_codes.astype(jnp.float32) / 1024.0
+    teacher = jnp.zeros((tokens.shape[0], D), jnp.float32)
+    for route in range(2):
+        picker = place[:, route, :].astype(jnp.bfloat16)
+        picked = jnp.dot(picker, results, preferred_element_type=jnp.float32)
+        teacher = teacher + weights[:, route][:, None] * picked
+    return (fake_score.astype(jnp.float32) - teacher).astype(jnp.bfloat16)
+
+
+def on_device_general(tokens, expert_ids, gate_codes, fake_score, gate_weight, up_weight, down_weight):
     slots_all = NE * CAP
     hits = expert_ids[:, :, None] == jnp.arange(NE)[None, None, :]
     routed = jnp.sum(hits.astype(jnp.int32), axis=1)
@@ -64,5 +116,5 @@
     )
     out_specs = P(("view", "expert", "col"), None)
     return jax.shard_map(
-        on_device, mesh=mesh, in_specs=in_specs, out_specs=out_specs, check_vma=False
+        on_device if mesh.shape["view"] == 2 else on_device_general, mesh=mesh, in_specs=in_specs, out_specs=out_specs, check_vma=False
     )

time: 395 us -> 309 us (0.78)
  waiting for transfers between devices: 286 us -> 199 us
  matrix products: 34.8 us -> 29.8 us
    all_gather x3 -> x0, waiting for transfers between devices: 154 us -> none  [the longest x1 53 us: on_device(): gate = add_rows(lax.all_gather(gate_weight, 'view', axis=1, tiled=True))]
    ppermute x0 -> x3, waiting for transfers between devices: none -> 71.2 us  [on_device(): lax.ppermute(w[0], 'view', swap)]
    dot_general x3 -> x6, matrix products: 30.4 us -> 26.5 us  [the longest x2 10.2 us: project(): jnp.dot(theirs, far, preferred_element_type=jnp.float32)]
  transfers between devices with their start and end apart: 6 -> 6, of which waited for: 6 -> 5; matrix products, arithmetic and copies ran while one was open for 7% -> 10% of each run, Pallas kernels for 0% -> 0%
where the time goes in v1:
time: 309 us
  waiting for transfers between devices  199 us (64%)
  blocking collectives  41.1 us (13%)
  matrix products  29.8 us (10%)
  between operations  13.6 us (4%)
  local copies, waits for them, and re-layouts  11.1 us (4%)
  starting transfers between devices  8.23 us (3%)
  other arithmetic  5.91 us (2%)
    ppermute x3, waiting for transfers between devices, on_device(): lax.ppermute(w[0], 'view', swap)  71.2 us
    reduce_scatter x1, waiting for transfers between devices, on_device(): lax.psum_scatter(partial_out, 'col', scatter_dimension=0, tiled=True)  53 us
    all_to_all x1, blocking collectives, on_device(): lax.all_to_all(outgoing.reshape(NE, CAP, D), 'expert', split_axis=0, conc...  41.1 us
    all_gather x1, waiting for transfers between devices, on_device(): gathered = lax.all_gather(arrived, 'col', axis=0, tiled=True)  39.8 us
    all_to_all x1, waiting for transfers between devices, on_device(): lax.all_to_all(summed.reshape(NE, CAP, D), 'expert', split_axis=0, concat...  34.8 us
    dot_general x2, matrix products, project(): jnp.dot(theirs, far, preferred_element_type=jnp.float32)  10.2 us
    dot_general x2, matrix products, project(): jnp.dot(mine, own, preferred_element_type=jnp.float32)  8.11 us
    reshape x1, local copies, waits for them, and re-layouts, on_device(): inputs = gathered.reshape(-1, D)  7.91 us
  transfers between devices with their start and end apart: 6, of which 5 were waited for; matrix products, arithmetic and copies ran while one was open for 10% of the time, Pallas kernels for 0%

profile of v1, /device:TPU:0, one launch (start us, length us, event | category | flops | bytes accessed | tf_op | source)
XLA Modules:
  0.0 308.6 jit_solution(13128853927263166412)
XLA Ops:
  6.5 0.0 copy-start
  6.5 0.0 all-gather.2.cloned.1.call-start
  6.5 0.8 convert_reduce_fusion
  7.3 0.1 copy.12
  7.4 0.2 reduce_window_sum.11
  7.6 0.1 copy.14
  7.7 0.7 select_reduce_fusion
  8.4 0.7 multiply_add_fusion
  9.1 0.7 iota_compare_fusion
  9.8 0.0 copy-done
  9.8 0.5 convolution_convert_fusion.2
  10.3 0.3 reshape.23
  10.6 41.1 %all_to_all.10 = bf16[4,68,2560]{2,1,0:T(8,128)(2,1)} all-to-all(bf16[4,68,2560]{2,1,0:T(8,128)(2,1)S(1)} %reshape.23), channel_id=1, replica_groups=mesh['view'=2,'expert'=4,'col'=4] {'expert'}, dimensions={0} | all-to-all | bytes 2785280 | tf_op jit(solution)/shard_map/all_to_all | solution.py:25
  51.7 0.0 all-gather.2.cloned.1.call-update
  51.7 0.0 reduce-scatter.2.cloned.1.call-start
  51.8 1.6 collective-permute-start
  53.3 0.5 collective-permute-start.1
  53.9 1.5 collective-permute-start.2
  55.4 0.0 copy-start.5
  55.4 39.8 %all-gather.2.cloned.1.call-done = bf16[16,68,2560]{2,1,0:T(8,128)(2,1)} async-done(((bf16[4,68,2560]{2,1,0:T(8,128)(2,1)}), bf16[16,68,2560]{2,1,0:T(8,128)(2,1)}) %all-gather.2.cloned.1.call-update) | async-done | bytes 5570576 | tf_op jit(solution)/shard_map/all_gather | solution.py:28
  95.2 7.9 %reshape.24 = bf16[1088,2560]{1,0:T(8,128)(2,1)} reshape(bf16[16,68,2560]{2,1,0:T(8,128)(2,1)} %all-gather.2.cloned.1.call-done) | data formatting | bytes 11141120 | tf_op jit(solution)/shard_map/reshape | solution.py:29
  103.1 0.0 copy-done.5
  103.1 0.0 copy-start.1
  103.1 5.0 %fusion.9 = f32[1088,864]{1,0:T(8,128)S(1)} fusion(bf16[1088,2560]{1,0:T(8,128)(2,1)} %reshape.24, s32[]{:T(128)S(6)} %select_n.24, bf16[1,1280,864]{1,2,0:T(8,128)(2,1)S(1)} %copy-done.5), kind=kOutput, calls=%fused_computation.19 | convolution fusion | flops 2406481920 | bytes 8757252 | tf_op jit(solution)/shard_map/dot_general | solution.py:34
  108.1 0.0 copy-start.6
  108.1 0.0 collective-permute-done
  108.1 0.0 copy-done.1
  108.1 5.0 %convolution_add_fusion.1 = f32[1088,864]{1,0:T(8,128)S(1)} fusion(f32[1088,864]{1,0:T(8,128)S(1)} %fusion.9, bf16[1280,864]{0,1:T(8,128)(2,1)} %collective-permute-done, bf16[1088,2560]{1,0:T(8,128)(2,1)S(1)} %copy-done.1, s32[]{:T(128)S(6)} %select_n.25), kind=kOutput, calls=%fused_computation.5 | convolution fusion | flops 2407421952 | bytes 12656644 | tf_op jit(solution)/shard_map/dot_general | solution.py:34
  113.1 0.0 copy-done.6
  113.1 3.1 %fusion.7 = f32[1088,864]{1,0:T(8,128)S(1)} fusion(bf16[1088,2560]{1,0:T(8,128)(2,1)S(1)} %copy-done.1, s32[]{:T(128)S(6)} %select_n.24, bf16[1,1280,864]{1,2,0:T(8,128)(2,1)S(1)} %copy-done.6), kind=kOutput, calls=%fused_computation.17 | convolution fusion | flops 2406481920 | bytes 8757252 | tf_op jit(solution)/shard_map/dot_general | solution.py:34
  116.2 0.0 copy-start.7
  116.2 34.3 %collective-permute-done.1 = bf16[1280,864]{0,1:T(8,128)(2,1)} collective-permute-done((bf16[1280,864]{0,1:T(8,128)(2,1)}, bf16[1280,864]{0,1:T(8,128)(2,1)}, u32[]{:S(2)}, u32[]{:S(2)}) %collective-permute-start.1) | collective-permute-done | bytes 2211872 | tf_op jit(solution)/shard_map/ppermute | solution.py:24
  150.6 5.3 %fusion.4 = bf16[1088,864]{1,0:T(8,128)(2,1)S(1)} fusion(f32[1088,864]{1,0:T(8,128)S(1)} %fusion.7, bf16[1280,864]{0,1:T(8,128)(2,1)} %collective-permute-done.1, f32[1088,864]{1,0:T(8,128)S(1)} %convolution_add_fusion.1, bf16[1088,2560]{1,0:T(8,128)(2,1)S(1)} %copy-done.1, s32[]{:T(128)S(6)} %select_n.25), kind=kOutput, calls=%fused_computation.12 | convolution fusion | flops 2413062144 | bytes 14675972 | tf_op jit(solution)/shard_map/dot_general | solution.py:34
  155.8 0.0 copy-done.7
  155.9 3.3 %convolution_convert_fusion.1 = bf16[1088,1280]{1,0:T(8,128)(2,1)S(1)} fusion(bf16[1088,864]{1,0:T(8,128)(2,1)S(1)} %fusion.4, bf16[1,864,1280]{2,1,0:T(8,128)(2,1)S(1)} %copy-done.7), kind=kOutput, calls=%fused_computation.1 | convolution fusion | flops 2407874560 | bytes 6877184 | tf_op jit(solution)/shard_map/dot_general | solution.py:41
  159.1 36.8 %collective-permute-done.2 = bf16[864,1280]{1,0:T(8,128)(2,1)} collective-permute-done((bf16[864,1280]{1,0:T(8,128)(2,1)}, bf16[864,1280]{1,0:T(8,128)(2,1)}, u32[]{:S(2)}, u32[]{:S(2)}) %collective-permute-start.2) | collective-permute-done | bytes 2211872 | tf_op jit(solution)/shard_map/ppermute | solution.py:24
  195.9 4.9 %broadcast_select_fusion.1 = (bf16[1088,1280]{1,0:T(8,128)(2,1)S(1)}, bf16[1088,1280]{1,0:T(8,128)(2,1)S(1)}) fusion(bf16[1088,1280]{1,0:T(8,128)(2,1)S(1)} %convolution_convert_fusion.1, pred[]{:T(512)S(6)} %eq.36, bf16[1088,864]{1,0:T(8,128)(2,1)S(1)} %fusion.4, bf16[864,1280]{1,0:T(8,128)(2,1)} %collective-permute-done.2), kind=kOutput, calls=%fused_computation.14 | convolution fusion | flops 2410659840 | bytes 12447745 | tf_op jit(solution)/shard_map/dot_general | solution.py:42
  200.9 2.9 pad_maximum_fusion
  203.7 0.0 reduce-scatter.2.cloned.1.call-update
  203.7 0.0 copy-start.4
  203.8 53.0 %reduce-scatter.2.cloned.1.call-done = bf16[272,2560]{1,0:T(8,128)(2,1)} async-done(((bf16[1088,2560]{1,0:T(8,128)(2,1)}), bf16[272,2560]{1,0:T(8,128)(2,1)}) %reduce-scatter.2.cloned.1.call-update) | async-done | bytes 1392656 | tf_op jit(solution)/shard_map/reduce_scatter | solution.py:47
  256.7 2.4 reshape.25
  259.1 4.6 %all-to-all-start.1 = ((bf16[4,68,2560]{2,1,0:T(8,128)(2,1)}), bf16[4,68,2560]{2,1,0:T(8,128)(2,1)S(1)}, u32[]{:S(2)}, u32[]{:S(2)}) async-start(bf16[4,68,2560]{2,1,0:T(8,128)(2,1)} %reshape.25), calls=%async_computation.2 | async-start | bytes 2949120 | tf_op jit(solution)/shard_map/all_to_all | solution.py:50
  263.7 0.0 copy-done.4
  263.7 34.8 %all-to-all-done.1 = bf16[4,68,2560]{2,1,0:T(8,128)(2,1)S(1)} async-done(((bf16[4,68,2560]{2,1,0:T(8,128)(2,1)}), bf16[4,68,2560]{2,1,0:T(8,128)(2,1)S(1)}, u32[]{:S(2)}, u32[]{:S(2)}) %all-to-all-start.1) | async-done | bytes 1392672 | tf_op jit(solution)/shard_map/all_to_all | solution.py:50
  298.6 0.3 reshape.26
  298.9 0.0 copy-start.2
  298.9 0.0 copy-start.3
  298.9 1.4 convolution_multiply_fusion.1
  300.3 0.0 copy-done.2
  300.3 0.0 copy-done.3
  300.3 1.4 fusion.3
  (3 shorter events, 0.0 us)
Async XLA Ops:
  6.5 3.2 %copy-start = (bf16[128,2560]{1,0:T(8,128)(2,1)S(1)}, bf16[128,2560]{1,0:T(8,128)(2,1)}, u32[]{:S(2)}) copy-start(bf16[128,2560]{1,0:T(8,128)(2,1)} %param.7) | copy-start | bytes 1966084
  6.5 88.6 %all-gather.2.cloned.1.call-start = ((), (), s32[]{:S(2)}) async-start(), calls=%async_computation.3 | async-start | bytes 7372800 | tf_op jit(solution)/shard_map/all_gather | solution.py:28
  51.7 205.0 %reduce-scatter.2.cloned.1.call-start = ((), (), s32[]{:S(2)}) async-start(), calls=%async_computation.4 | async-start | bytes 6963200 | tf_op jit(solution)/shard_map/reduce_scatter | solution.py:47
  51.8 56.4 %collective-permute-start = (bf16[1280,864]{0,1:T(8,128)(2,1)}, bf16[1280,864]{0,1:T(8,128)(2,1)}, u32[]{:S(2)}, u32[]{:S(2)}) collective-permute-start(bf16[1280,864]{0,1:T(8,128)(2,1)} %bitcast.28), channel_id=1, source_target_pairs={{0,16},{16,0},{1,17},{17,1},{2,18},{18,2},{3,19},{19,3},{4,20},{20... | collective-permute-start | bytes 6635528 | tf_op jit(solution)/shard_map/ppermute | solution.py:24
  53.3 97.2 %collective-permute-start.1 = (bf16[1280,864]{0,1:T(8,128)(2,1)}, bf16[1280,864]{0,1:T(8,128)(2,1)}, u32[]{:S(2)}, u32[]{:S(2)}) collective-permute-start(bf16[1280,864]{0,1:T(8,128)(2,1)} %bitcast.29), channel_id=1, source_target_pairs={{0,16},{16,0},{1,17},{17,1},{2,18},{18,2},{3,19},{19,3},{4,20},{20... | collective-permute-start | bytes 6635528 | tf_op jit(solution)/shard_map/ppermute | solution.py:24
  53.9 142.1 %collective-permute-start.2 = (bf16[864,1280]{1,0:T(8,128)(2,1)}, bf16[864,1280]{1,0:T(8,128)(2,1)}, u32[]{:S(2)}, u32[]{:S(2)}) collective-permute-start(bf16[864,1280]{1,0:T(8,128)(2,1)} %bitcast.30), channel_id=1, source_target_pairs={{0,16},{16,0},{1,17},{17,1},{2,18},{18,2},{3,19},{19,3},{4,20},{20... | collective-permute-start | bytes 6635528 | tf_op jit(solution)/shard_map/ppermute | solution.py:24
  55.4 47.7 %copy-start.5 = (bf16[1,1280,864]{1,2,0:T(8,128)(2,1)S(1)}, bf16[1,1280,864]{1,2,0:T(8,128)(2,1)}, u32[]{:S(2)}) copy-start(bf16[1,1280,864]{1,2,0:T(8,128)(2,1)} %param.11) | copy-start | bytes 6635524
  103.1 5.1 %copy-start.1 = (bf16[1088,2560]{1,0:T(8,128)(2,1)S(1)}, bf16[1088,2560]{1,0:T(8,128)(2,1)}, u32[]{:S(2)}) copy-start(bf16[1088,2560]{1,0:T(8,128)(2,1)} %reshape.24) | copy-start | bytes 16711684
  108.1 5.0 %copy-start.6 = (bf16[1,1280,864]{1,2,0:T(8,128)(2,1)S(1)}, bf16[1,1280,864]{1,2,0:T(8,128)(2,1)}, u32[]{:S(2)}) copy-start(bf16[1,1280,864]{1,2,0:T(8,128)(2,1)} %param.12) | copy-start | bytes 6635524
  116.2 39.6 %copy-start.7 = (bf16[1,864,1280]{2,1,0:T(8,128)(2,1)S(1)}, bf16[1,864,1280]{2,1,0:T(8,128)(2,1)}, u32[]{:S(2)}) copy-start(bf16[1,864,1280]{2,1,0:T(8,128)(2,1)} %param.13) | copy-start | bytes 6635524
  203.7 59.9 %copy-start.4 = (s32[128,2]{0,1:T(2,128)S(1)}, s32[128,2]{0,1:T(2,128)}, u32[]{:S(2)}) copy-start(s32[128,2]{0,1:T(2,128)} %param.9) | copy-start | bytes 3076
  259.1 39.5 %all-to-all-start.1 = ((bf16[4,68,2560]{2,1,0:T(8,128)(2,1)}), bf16[4,68,2560]{2,1,0:T(8,128)(2,1)S(1)}, u32[]{:S(2)}, u32[]{:S(2)}) async-start(bf16[4,68,2560]{2,1,0:T(8,128)(2,1)} %reshape.25), calls=%async_computation.2 | async-start | bytes 2949120 | tf_op jit(solution)/shard_map/all_to_all | solution.py:50
  298.9 1.4 copy-start.2
  298.9 1.4 copy-start.3
Sparse Core Ops, SparseCore 0:
  51.8 43.2 all-gather.1
  203.9 52.8 reduce-scatter.1

commit v2 on v0

--- a/solution.py
+++ b/solution.py
@@ -1,11 +1,327 @@
+import functools
+
 import jax
 import jax.numpy as jnp
 from jax import lax
+from jax.experimental import pallas as pl
+from jax.experimental.pallas import tpu as pltpu
 from jax.sharding import PartitionSpec as P
 
 D = 2560
 NE = 4
 CAP = 68
+PAIR = 144
+F32 = jnp.float32
+BF16 = jnp.bfloat16
+NEAR = (((1,), (1,)), ((), ()))
+
+
+def fused(ids_ref, codes_ref, tok_ref, fake_ref, wg_ref, wu_ref, wd_ref, out_ref,
+          near_g, near_u, far_g, far_u, down, x, sent_z, gate, up, hidden,
+          place, sib_place, sib_tok, sib_fake, combine,
+          part, core_in, pair_sum, y_in, y_sum, back, sib_gap, gap_in,
+          far_send, far_recv, down_send, down_recv, near_sem, near_down,
+          sib_send, sib_recv, z_send, z_recv, y_send, y_recv, c_send, c_recv,
+          a_send, a_recv, b_send, b_recv, e_send, e_recv, g_send, g_recv):
+    v, e, c = lax.axis_index("view"), lax.axis_index("expert"), lax.axis_index("col")
+    k, y = c % 2, c // 2
+    half = D // 2
+    chunks = down.shape[0]
+    per_view = chunks // 2
+    wide = down.shape[2]
+    lane = wide // 2
+    tokens = tok_ref.shape[0]
+    blocks = gate.shape[0]
+    rows = gate.shape[1]
+    ff = gate.shape[2]
+    to_view = (1 - v, e, c)
+    to_sib = (v, e, y * 2 + 1 - k)
+    to_y = (v, e, (1 - y) * 2 + k)
+
+    def remote(src, dst, send, recv, device):
+        return pltpu.make_async_remote_copy(
+            src_ref=src, dst_ref=dst, send_sem=send, recv_sem=recv,
+            device_id=device, device_id_type=pl.DeviceIdType.MESH)
+
+    def expert_at(step):
+        return (e + step) % NE
+
+    barrier = pltpu.get_barrier_semaphore()
+    others = [to_view, to_sib, to_y] + [(v, expert_at(s), c) for s in range(1, NE)]
+    for device in others:
+        pl.semaphore_signal(barrier, inc=1, device_id=device, device_id_type=pl.DeviceIdType.MESH)
+    pl.semaphore_wait(barrier, len(others))
+
+    send_g = remote(wg_ref, far_g, far_send.at[0], far_recv.at[0], to_view)
+    send_u = remote(wu_ref, far_u, far_send.at[1], far_recv.at[1], to_view)
+    send_g.start()
+    send_u.start()
+    send_tok = remote(tok_ref.at[:, pl.ds(pl.multiple_of((1 - k) * half, half), half)], sib_tok,
+                      sib_send.at[0], sib_recv.at[0], to_sib)
+    send_tok.start()
+    send_fake = remote(fake_ref, sib_fake, sib_send.at[1], sib_recv.at[1], to_sib)
+    send_fake.start()
+    own_g = pltpu.make_async_copy(wg_ref, near_g, near_sem.at[0])
+    own_u = pltpu.make_async_copy(wu_ref, near_u, near_sem.at[1])
+    own_g.start()
+    own_u.start()
+
+    def own_down(j):
+        return pltpu.make_async_copy(
+            wd_ref.at[:, pl.ds(pl.multiple_of(j * wide, wide), wide)], down.at[j], near_down.at[j])
+
+    def far_down(j):
+        return remote(wd_ref.at[:, pl.ds(pl.multiple_of(j * wide, wide), wide)],
+                      down.at[per_view + j], down_send.at[j], down_recv.at[j], to_view)
+
+    for j in range(per_view):
+        own_down(j).start()
+
+    id0, id1 = ids_ref[0:1, :], ids_ref[1:2, :]
+    which = lax.broadcasted_iota(jnp.int32, (16, tokens), 0)
+    hits = jnp.where((which == id0) | (which == id1), 1.0, 0.0).astype(BF16)
+    earlier = jnp.where(
+        lax.broadcasted_iota(jnp.int32, (tokens, tokens), 0)
+        < lax.broadcasted_iota(jnp.int32, (tokens, tokens), 1), 1.0, 0.0).astype(BF16)
+    before = jnp.dot(hits, earlier, preferred_element_type=F32)
+    slot0 = jnp.sum(jnp.where(which == id0, before, 0.0), axis=0, keepdims=True).astype(jnp.int32)
+    slot1 = jnp.sum(jnp.where(which == id1, before, 0.0), axis=0, keepdims=True).astype(jnp.int32)
+    row = lax.broadcasted_iota(jnp.int32, (NE * PAIR, tokens), 0)
+    is0 = row == id0 * PAIR + k * CAP + slot0
+    is1 = row == id1 * PAIR + k * CAP + slot1
+    code0, code1 = codes_ref[0:1, :], codes_ref[1:2, :]
+    hi0, hi1 = (code0 // 32).astype(F32) / 32.0, (code1 // 32).astype(F32) / 32.0
+    lo0, lo1 = (code0 % 32).astype(F32) / 1024.0, (code1 % 32).astype(F32) / 1024.0
+    hi = jnp.where(is0, hi0, 0.0) + jnp.where(is1, hi1, 0.0)
+    lo = jnp.where(is0, lo0, 0.0) + jnp.where(is1, lo1, 0.0)
+    place[0] = hi.astype(BF16)
+    place[1] = lo.astype(BF16)
+    send_place = remote(place, sib_place, sib_send.at[2], sib_recv.at[2], to_sib)
+    send_place.start()
+    select = jnp.where(is0 | is1, 1.0, 0.0).astype(BF16)
+    mine = jnp.dot(select, tok_ref[:, pl.ds(pl.multiple_of(k * half, half), half)],
+                   preferred_element_type=F32)
+    send_tok.wait_recv()
+    send_place.wait_recv()
+    sib_hi, sib_lo = sib_place[0].astype(F32), sib_place[1].astype(F32)
+    sib_select = jnp.where(sib_hi + sib_lo > 0.0, 1.0, 0.0).astype(BF16)
+    both = mine + jnp.dot(sib_select, sib_tok[...], preferred_element_type=F32)
+    sent_z[...] = both.astype(BF16).reshape(NE, PAIR, half)
+    x[k, y, e] = sent_z[e]
+
+    def z_copy(s):
+        peer = expert_at(s)
+        return remote(sent_z.at[peer], x.at[k, y, e], z_send.at[s - 1], z_recv.at[s - 1], (v, peer, c))
+
+    def z_arrived(s):
+        return remote(sent_z.at[0], x.at[k, y, expert_at(NE - s)], z_send.at[s - 1], z_recv.at[s - 1], to_view)
+
+    def y_copy(s):
+        at = x.at[k, y, expert_at(NE - s)]
+        return remote(at, at, y_send.at[s], y_recv.at[s], to_y)
+
+    def y_arrived(s):
+        at = x.at[k, 1 - y, expert_at(NE - s)]
+        return remote(at, at, y_send.at[s], y_recv.at[s], to_y)
+
+    def c_copy(s, far):
+        at = x.at[k, (1 - y) if far else y, expert_at(NE - s)]
+        return remote(at, at, c_send.at[far, s], c_recv.at[far, s], to_sib)
+
+    def c_arrived(s, far):
+        at = x.at[1 - k, (1 - y) if far else y, expert_at(NE - s)]
+        return remote(at, at, c_send.at[far, s], c_recv.at[far, s], to_sib)
+
+    for s in range(1, NE):
+        z_copy(s).start()
+    y_copy(0).start()
+    c_copy(0, 0).start()
+    combine[0, 0:tokens] = hi.T.astype(BF16)
+    combine[1, 0:tokens] = lo.T.astype(BF16)
+    combine[0, tokens:2 * tokens] = sib_hi.T.astype(BF16)
+    combine[1, tokens:2 * tokens] = sib_lo.T.astype(BF16)
+    for s in range(1, NE):
+        z_arrived(s).wait_recv()
+        y_copy(s).start()
+        c_copy(s, 0).start()
+    for s in range(NE):
+        y_arrived(s).wait_recv()
+        c_copy(s, 1).start()
+    for far in range(2):
+        for s in range(NE):
+            c_arrived(s, far).wait_recv()
+
+    def x_rows(view, i):
+        return x[view, i // 2, pl.ds((i % 2) * 2, 2)].reshape(rows, half)
+
+    own_g.wait()
+    own_u.wait()
+
+    @pl.loop(0, blocks)
+    def _(i):
+        gate[i] = lax.dot_general(x_rows(v, i), near_g[...], NEAR, preferred_element_type=F32)
+        up[i] = lax.dot_general(x_rows(v, i), near_u[...], NEAR, preferred_element_type=F32)
+
+    send_g.wait_recv()
+
+    @pl.loop(0, blocks)
+    def _(i):
+        gate[i] += lax.dot_general(x_rows(1 - v, i), far_g[...], NEAR, preferred_element_type=F32)
+
+    send_u.wait_recv()
+    far_down(0).start()
+    far_down(1).start()
+
+    @pl.loop(0, blocks)
+    def _(i):
+        u = up[i] + lax.dot_general(x_rows(1 - v, i), far_u[...], NEAR, preferred_element_type=F32)
+        g = gate[i]
+        hidden[i] = (g / (1.0 + jnp.exp(-g)) * u).astype(BF16)
+
+    def stage_a(j):
+        return remote(part.at[j, 1 - k], core_in.at[j], a_send.at[j], a_recv.at[j], to_sib)
+
+    def stage_b(j):
+        return remote(pair_sum.at[j, 1 - y], y_in.at[j], b_send.at[j], b_recv.at[j], to_y)
+
+    def stage_c(j, s):
+        peer = expert_at(s)
+        return remote(y_sum.at[j, peer], back.at[j, e], e_send.at[s - 1, j], e_recv.at[s - 1, j], (v, peer, c))
+
+    def stage_c_in(j, s):
+        return remote(y_sum.at[j, 0], back.at[j, expert_at(NE - s)], e_send.at[s - 1, j], e_recv.at[s - 1, j], to_view)
+
+    def stage_d(j):
+        return remote(sib_gap.at[j], gap_in.at[j], g_send.at[j], g_recv.at[j], to_sib)
+
+    def columns(j, core):
+        first = (j // per_view + v) % 2 * half + (j % per_view) * wide + core * lane
+        return pl.ds(pl.multiple_of(first, lane), lane)
+
+    send_fake.wait_recv()
+
+    @pl.loop(0, chunks + 3)
+    def _(t):
+        @pl.when(t < per_view)
+        def _():
+            own_down(t).wait()
+
+        @pl.when((t >= per_view) & (t < chunks))
+        def _():
+            far_down(t - per_view).wait_recv()
+
+        @pl.when((t >= per_view) & (t < chunks - 2))
+        def _():
+            far_down(t - per_view + 2).start()
+
+        @pl.when(t < chunks)
+        def _():
+            @pl.loop(0, blocks)
+            def _(i):
+                p = jnp.dot(hidden[i], down[t], preferred_element_type=F32).astype(BF16)
+                at = pl.ds(pl.multiple_of(i * rows, rows), rows)
+                part[t, 0, at, :] = p[:, :lane]
+                part[t, 1, at, :] = p[:, lane:]
+            stage_a(t).start()
+
+        @pl.when((t >= 1) & (t < chunks + 1))
+        def _():
+            j = t - 1
+            stage_a(j).wait_recv()
+            total = part[j, k].astype(F32) + core_in[j].astype(F32)
+            pair_sum[j] = total.astype(BF16).reshape(2, NE * PAIR, lane)
+            stage_b(j).start()
+
+        @pl.when((t >= 2) & (t < chunks + 2))
+        def _():
+            j = t - 2
+            stage_b(j).wait_recv()
+            total = pair_sum[j, y].astype(F32) + y_in[j].astype(F32)
+            y_sum[j] = total.astype(BF16).reshape(NE, PAIR, lane)
+            for s in range(1, NE):
+                stage_c(j, s).start()
+            back[j, e] = y_sum[j, e]
+
+        @pl.when(t >= 3)
+        def _():
+            j = t - 3
+            for s in range(1, NE):
+                stage_c_in(j, s).wait_recv()
+            result = back[j].reshape(NE * PAIR, lane)
+            teacher = jnp.dot(combine[0], result, preferred_element_type=F32) + jnp.dot(
+                combine[1], result, preferred_element_type=F32)
+            at = columns(j, k)
+            sib_gap[j] = (sib_fake[:, at].astype(F32) - teacher[tokens:]).astype(BF16)
+            stage_d(j).start()
+            out_ref[:, at] = (fake_ref[:, at].astype(F32) - teacher[:tokens]).astype(BF16)
+
+    @pl.loop(0, chunks)
+    def _(j):
+        stage_d(j).wait_recv()
+        out_ref[:, columns(j, 1 - k)] = gap_in[j]
+        stage_a(j).wait_send()
+        stage_b(j).wait_send()
+        for s in range(1, NE):
+            stage_c(j, s).wait_send()
+        stage_d(j).wait_send()
+
+    for j in range(per_view):
+        far_down(j).wait_send()
+    for copy in (send_g, send_u, send_tok, send_fake, send_place):
+        copy.wait_send()
+    for s in range(1, NE):
+        z_copy(s).wait_send()
+    for s in range(NE):
+        y_copy(s).wait_send()
+        c_copy(s, 0).wait_send()
+        c_copy(s, 1).wait_send()
+
+
+def on_device_fused(tokens, expert_ids, gate_codes, fake_score, gate_weight, up_weight, down_weight):
+    ff, half = gate_weight.shape[2], gate_weight.shape[1]
+    count = tokens.shape[0]
+    chunks, wide, lane = 10, 256, 128
+    total = 8 * PAIR
+    dma = pltpu.SemaphoreType.DMA
+    vmem = pl.BlockSpec(memory_space=pltpu.VMEM)
+    anywhere = pl.BlockSpec(memory_space=pl.ANY)
+    return pl.pallas_call(
+        fused,
+        out_shape=jax.ShapeDtypeStruct((count, D), BF16),
+        in_specs=[vmem] * 4 + [anywhere] * 3,
+        out_specs=vmem,
+        scratch_shapes=[
+            pltpu.VMEM((ff, half), BF16), pltpu.VMEM((ff, half), BF16),
+            pltpu.VMEM((ff, half), BF16), pltpu.VMEM((ff, half), BF16),
+            pltpu.VMEM((chunks, ff, wide), BF16),
+            pltpu.VMEM((2, 2, NE, PAIR, half), BF16),
+            pltpu.VMEM((NE, PAIR, half), BF16),
+            pltpu.VMEM((4, total // 4, ff), F32), pltpu.VMEM((4, total // 4, ff), F32),
+            pltpu.VMEM((4, total // 4, ff), BF16),
+            pltpu.VMEM((2, NE * PAIR, count), BF16), pltpu.VMEM((2, NE * PAIR, count), BF16),
+            pltpu.VMEM((count, half), BF16), pltpu.VMEM((count, D), BF16),
+            pltpu.VMEM((2, 2 * count, NE * PAIR), BF16),
+            pltpu.VMEM((chunks, 2, total, lane), BF16),
+            pltpu.VMEM((chunks, total, lane), BF16),
+            pltpu.VMEM((chunks, 2, NE * PAIR, lane), BF16),
+            pltpu.VMEM((chunks, NE * PAIR, lane), BF16),
+            pltpu.VMEM((chunks, NE, PAIR, lane), BF16),
+            pltpu.VMEM((chunks, NE, PAIR, lane), BF16),
+            pltpu.VMEM((chunks, count, lane), BF16), pltpu.VMEM((chunks, count, lane), BF16),
+            dma((2,)), dma((2,)), dma((chunks // 2,)), dma((chunks // 2,)), dma((2,)), dma((chunks // 2,)),
+            dma((3,)), dma((3,)), dma((NE - 1,)), dma((NE - 1,)), dma((NE,)), dma((NE,)),
+            dma((2, NE)), dma((2, NE)),
+            dma((chunks,)), dma((chunks,)), dma((chunks,)), dma((chunks,)),
+            dma((NE - 1, chunks)), dma((NE - 1, chunks)), dma((chunks,)), dma((chunks,)),
+        ],
+        compiler_params=pltpu.CompilerParams(
+            collective_id=0, has_side_effects=True, vmem_limit_bytes=60 * 1024 * 1024),
+        cost_estimate=pl.CostEstimate(
+            flops=6 * total * D * ff, bytes_accessed=6 * D * ff, transcendentals=total * ff),
+    )(
+        expert_ids.T, gate_codes.T, tokens, fake_score,
+        gate_weight[0].T, up_weight[0].T, down_weight[0],
+    )
 
 
 def on_device(tokens, expert_ids, gate_codes, fake_score, gate_weight, up_weight, down_weight):
@@ -64,5 +380,5 @@
     )
     out_specs = P(("view", "expert", "col"), None)
     return jax.shard_map(
-        on_device, mesh=mesh, in_specs=in_specs, out_specs=out_specs, check_vma=False
-    )
+        on_device_fused if mesh.shape["view"] == 2 else on_device, mesh=mesh, in_specs=in_specs, out_specs=out_specs, check_vma=False
+    )

time: 395 us -> 171 us (0.43)
  waiting for transfers between devices: 286 us -> 0 us
  Pallas kernels: 0 us -> 169 us
  blocking collectives: 41.1 us -> 0 us
  matrix products: 34.8 us -> 0 us
  between operations: 13.2 us -> 0.01 us
  local copies, waits for them, and re-layouts: 11.1 us -> 1.97 us
  starting transfers between devices: 4.76 us -> 0 us
    all_gather x4 -> x0, waiting for transfers between devices: 196 us -> none  [the longest x1 53 us: on_device(): gate = add_rows(lax.all_gather(gate_weight, 'view', axis=1, tiled=True))]
    pallas_call x0 -> x1, Pallas kernels: none -> 169 us  [on_device_fused(): pl.pallas_call(fused, out_shape=jax.ShapeDtypeStruct((count, D), BF16), i...]
    reduce_scatter x1 -> x0, waiting for transfers between devices: 53.7 us -> none  [on_device(): lax.psum_scatter(partial_out.astype(jnp.bfloat16), 'col', scatter_dimensi...]
    all_to_all x1 -> x0, blocking collectives: 41.1 us -> none  [on_device(): lax.all_to_all(outgoing.reshape(NE, CAP, D), 'expert', split_axis=0, conc...]
    all_to_all x1 -> x0, waiting for transfers between devices: 34.8 us -> none  [on_device(): lax.all_to_all(summed.reshape(NE, CAP, D), 'expert', split_axis=0, concat...]
    dot_general x6 -> x0, matrix products: 34.8 us -> none  [the longest x2 20.4 us: add_rows(): return jnp.dot(inputs, piece[0], preferred_element_type=jnp.float32)]
    reshape x4 -> x0, local copies, waits for them, and re-layouts: 10.9 us -> none  [the longest x1 7.92 us: on_device(): inputs = gathered.reshape(-1, D)]
    all_to_all x1 -> x0, starting transfers between devices: 4.6 us -> none  [on_device(): lax.all_to_all(summed.reshape(NE, CAP, D), 'expert', split_axis=0, concat...]
  transfers between devices with their start and end apart: 6 -> 0, of which waited for: 6 -> 0; matrix products, arithmetic and copies ran while one was open for 7% -> 0% of each run, Pallas kernels for 0% -> 0%
where the time goes in v2:
time: 171 us
  Pallas kernels  169 us (99%)
  local copies, waits for them, and re-layouts  1.97 us (1%)
    pallas_call x1, Pallas kernels, on_device_fused(): pl.pallas_call(fused, out_shape=jax.ShapeDtypeStruct((count, D), BF16), i...  169 us

profile of v2, /device:TPU:0, one launch (start us, length us, event | category | flops | bytes accessed | tf_op | source)
XLA Modules:
  0.0 170.9 jit_solution(13841702316188078379)
XLA Ops:
  0.0 169.0 %shard_map.73 = bf16[128,2560]{1,0:T(8,128)(2,1)} custom-call(s32[2,128]{1,0:T(2,128)} %bitcast.12, s32[2,128]{1,0:T(2,128)} %bitcast.13, bf16[128,2560]{1,0:T(8,128)(2,1)} %tok_ref.1, bf16[128,2560]{1,0:T(8,128)(2,1)} %fake_ref.1, bf16[864,1280]{1,0:T(8,128)(2,1)} %bitcast.9, bf16[864,1280]{1,0:T(8,128)(2,1)} %bitcast.10, bf16[864,1280]{1,0:T(8,128)(2,1)} %bitcast.11), custom_call_target="tpu_custom_call" | custom-call | flops 15288238080 | bytes 13271040 | tf_op jit(solution)/shard_map/pallas_call | solution.py:288
  169.0 2.0 %copy.9 = bf16[128,2560]{1,0:T(8,128)(2,1)} copy(bf16[128,2560]{1,0:T(8,128)(2,1)} %shard_map.73) | data formatting | bytes 1310720

commit v3 on v2

--- a/solution.py
+++ b/solution.py
@@ -168,9 +168,9 @@
     def _(i):
         gate[i] += lax.dot_general(x_rows(1 - v, i), far_g[...], NEAR, preferred_element_type=F32)
 
+    for j in range(per_view):
+        far_down(j).start()
     send_u.wait_recv()
-    far_down(0).start()
-    far_down(1).start()
 
     @pl.loop(0, blocks)
     def _(i):
@@ -202,28 +202,6 @@
 
     @pl.loop(0, chunks + 3)
     def _(t):
-        @pl.when(t < per_view)
-        def _():
-            own_down(t).wait()
-
-        @pl.when((t >= per_view) & (t < chunks))
-        def _():
-            far_down(t - per_view).wait_recv()
-
-        @pl.when((t >= per_view) & (t < chunks - 2))
-        def _():
-            far_down(t - per_view + 2).start()
-
-        @pl.when(t < chunks)
-        def _():
-            @pl.loop(0, blocks)
-            def _(i):
-                p = jnp.dot(hidden[i], down[t], preferred_element_type=F32).astype(BF16)
-                at = pl.ds(pl.multiple_of(i * rows, rows), rows)
-                part[t, 0, at, :] = p[:, :lane]
-                part[t, 1, at, :] = p[:, lane:]
-            stage_a(t).start()
-
         @pl.when((t >= 1) & (t < chunks + 1))
         def _():
             j = t - 1
@@ -254,6 +232,24 @@
             sib_gap[j] = (sib_fake[:, at].astype(F32) - teacher[tokens:]).astype(BF16)
             stage_d(j).start()
             out_ref[:, at] = (fake_ref[:, at].astype(F32) - teacher[:tokens]).astype(BF16)
+
+        @pl.when(t < per_view)
+        def _():
+            own_down(t).wait()
+
+        @pl.when((t >= per_view) & (t < chunks))
+        def _():
+            far_down(t - per_view).wait_recv()
+
+        @pl.when(t < chunks)
+        def _():
+            @pl.loop(0, blocks)
+            def _(i):
+                p = jnp.dot(hidden[i], down[t], preferred_element_type=F32).astype(BF16)
+                at = pl.ds(pl.multiple_of(i * rows, rows), rows)
+                part[t, 0, at, :] = p[:, :lane]
+                part[t, 1, at, :] = p[:, lane:]
+            stage_a(t).start()
 
     @pl.loop(0, chunks)
     def _(j):

time: 171 us -> 168 us (0.982)
  Pallas kernels: 169 us -> 166 us
    pallas_call x1, Pallas kernels: 169 us -> 166 us  [on_device_fused(): pl.pallas_call(fused, out_shape=jax.ShapeDtypeStruct((count, D), BF16), i...]
where the time goes in v3:
time: 168 us
  Pallas kernels  166 us (99%)
  local copies, waits for them, and re-layouts  1.97 us (1%)
    pallas_call x1, Pallas kernels, on_device_fused(): pl.pallas_call(fused, out_shape=jax.ShapeDtypeStruct((count, D), BF16), i...  166 us

profile of v3, /device:TPU:0, one launch (start us, length us, event | category | flops | bytes accessed | tf_op | source)
XLA Modules:
  0.0 167.5 jit_solution(5705449286229657426)
XLA Ops:
  0.0 165.6 %shard_map.73 = bf16[128,2560]{1,0:T(8,128)(2,1)} custom-call(s32[2,128]{1,0:T(2,128)} %bitcast.12, s32[2,128]{1,0:T(2,128)} %bitcast.13, bf16[128,2560]{1,0:T(8,128)(2,1)} %tok_ref.1, bf16[128,2560]{1,0:T(8,128)(2,1)} %fake_ref.1, bf16[864,1280]{1,0:T(8,128)(2,1)} %bitcast.9, bf16[864,1280]{1,0:T(8,128)(2,1)} %bitcast.10, bf16[864,1280]{1,0:T(8,128)(2,1)} %bitcast.11), custom_call_target="tpu_custom_call" | custom-call | flops 15288238080 | bytes 13271040 | tf_op jit(solution)/shard_map/pallas_call | solution.py:284
  165.6 2.0 %copy.9 = bf16[128,2560]{1,0:T(8,128)(2,1)} copy(bf16[128,2560]{1,0:T(8,128)(2,1)} %shard_map.73) | data formatting | bytes 1310720

commit v4 on v3

--- a/solution.py
+++ b/solution.py
@@ -178,11 +178,16 @@
         g = gate[i]
         hidden[i] = (g / (1.0 + jnp.exp(-g)) * u).astype(BF16)
 
-    def stage_a(j):
-        return remote(part.at[j, 1 - k], core_in.at[j], a_send.at[j], a_recv.at[j], to_sib)
-
-    def stage_b(j):
-        return remote(pair_sum.at[j, 1 - y], y_in.at[j], b_send.at[j], b_recv.at[j], to_y)
+    def block_at(i):
+        return pl.ds(pl.multiple_of(i * rows, rows), rows)
+
+    def stage_a(j, i):
+        at = block_at(i)
+        return remote(part.at[j, 1 - k, at], core_in.at[j, at], a_send.at[i, j], a_recv.at[i, j], to_sib)
+
+    def stage_b(j, piece):
+        at = block_at(piece)
+        return remote(pair_sum.at[j, 1 - y, at], y_in.at[j, at], b_send.at[piece, j], b_recv.at[piece, j], to_y)
 
     def stage_c(j, s):
         peer = expert_at(s)
@@ -205,19 +210,31 @@
         @pl.when((t >= 1) & (t < chunks + 1))
         def _():
             j = t - 1
-            stage_a(j).wait_recv()
-            total = part[j, k].astype(F32) + core_in[j].astype(F32)
-            pair_sum[j] = total.astype(BF16).reshape(2, NE * PAIR, lane)
-            stage_b(j).start()
+
+            def add_pair(line, piece):
+                stage_a(j, line * 2 + piece).wait_recv()
+                at = block_at(line * 2 + piece)
+                total = part[j, k, at].astype(F32) + core_in[j, at].astype(F32)
+                pair_sum[j, line, block_at(piece)] = total.astype(BF16)
+
+            for piece in range(2):
+                add_pair(1 - y, piece)
+                stage_b(j, piece).start()
+            for piece in range(2):
+                add_pair(y, piece)
 
         @pl.when((t >= 2) & (t < chunks + 2))
         def _():
             j = t - 2
-            stage_b(j).wait_recv()
-            total = pair_sum[j, y].astype(F32) + y_in[j].astype(F32)
-            y_sum[j] = total.astype(BF16).reshape(NE, PAIR, lane)
-            for s in range(1, NE):
-                stage_c(j, s).start()
+            for piece in range(2):
+                stage_b(j, piece).wait_recv()
+                at = block_at(piece)
+                total = pair_sum[j, y, at].astype(F32) + y_in[j, at].astype(F32)
+                y_sum[j, 2 * piece:2 * piece + 2] = total.astype(BF16).reshape(2, PAIR, lane)
+                for peer in (2 * piece, 2 * piece + 1):
+                    @pl.when(peer != e)
+                    def _():
+                        stage_c(j, (peer - e + NE) % NE).start()
             back[j, e] = y_sum[j, e]
 
         @pl.when(t >= 3)
@@ -226,12 +243,15 @@
             for s in range(1, NE):
                 stage_c_in(j, s).wait_recv()
             result = back[j].reshape(NE * PAIR, lane)
-            teacher = jnp.dot(combine[0], result, preferred_element_type=F32) + jnp.dot(
-                combine[1], result, preferred_element_type=F32)
             at = columns(j, k)
-            sib_gap[j] = (sib_fake[:, at].astype(F32) - teacher[tokens:]).astype(BF16)
+
+            def teacher(first):
+                return jnp.dot(combine[0, first:first + tokens], result, preferred_element_type=F32) + jnp.dot(
+                    combine[1, first:first + tokens], result, preferred_element_type=F32)
+
+            sib_gap[j] = (sib_fake[:, at].astype(F32) - teacher(tokens)).astype(BF16)
             stage_d(j).start()
-            out_ref[:, at] = (fake_ref[:, at].astype(F32) - teacher[:tokens]).astype(BF16)
+            out_ref[:, at] = (fake_ref[:, at].astype(F32) - teacher(0)).astype(BF16)
 
         @pl.when(t < per_view)
         def _():
@@ -244,19 +264,22 @@
         @pl.when(t < chunks)
         def _():
             @pl.loop(0, blocks)
-            def _(i):
+            def _(turn):
+                i = ((turn + 1 + y) % 2) * 2 + turn // 2
                 p = jnp.dot(hidden[i], down[t], preferred_element_type=F32).astype(BF16)
                 at = pl.ds(pl.multiple_of(i * rows, rows), rows)
                 part[t, 0, at, :] = p[:, :lane]
                 part[t, 1, at, :] = p[:, lane:]
-            stage_a(t).start()
+                stage_a(t, i).start()
 
     @pl.loop(0, chunks)
     def _(j):
         stage_d(j).wait_recv()
         out_ref[:, columns(j, 1 - k)] = gap_in[j]
-        stage_a(j).wait_send()
-        stage_b(j).wait_send()
+        for i in range(blocks):
+            stage_a(j, i).wait_send()
+        for piece in range(2):
+            stage_b(j, piece).wait_send()
         for s in range(1, NE):
             stage_c(j, s).wait_send()
         stage_d(j).wait_send()
@@ -307,11 +330,11 @@
             dma((2,)), dma((2,)), dma((chunks // 2,)), dma((chunks // 2,)), dma((2,)), dma((chunks // 2,)),
             dma((3,)), dma((3,)), dma((NE - 1,)), dma((NE - 1,)), dma((NE,)), dma((NE,)),
             dma((2, NE)), dma((2, NE)),
-            dma((chunks,)), dma((chunks,)), dma((chunks,)), dma((chunks,)),
+            dma((4, chunks)), dma((4, chunks)), dma((2, chunks)), dma((2, chunks)),
             dma((NE - 1, chunks)), dma((NE - 1, chunks)), dma((chunks,)), dma((chunks,)),
         ],
         compiler_params=pltpu.CompilerParams(
-            collective_id=0, has_side_effects=True, vmem_limit_bytes=60 * 1024 * 1024),
+            collective_id=0, has_side_effects=True, vmem_limit_bytes=57 * 1024 * 1024),
         cost_estimate=pl.CostEstimate(
             flops=6 * total * D * ff, bytes_accessed=6 * D * ff, transcendentals=total * ff),
     )(

time: 168 us -> 167 us (level)
  Pallas kernels: 166 us -> 164 us
where the time goes in v4:
time: 167 us; the launch traced here: 166 us
  Pallas kernels  164 us (98%)
  local copies, waits for them, and re-layouts  1.97 us (1%)
    pallas_call x1, Pallas kernels, on_device_fused(): pl.pallas_call(fused, out_shape=jax.ShapeDtypeStruct((count, D), BF16), i...  164 us

profile of v4, /device:TPU:0, one launch (start us, length us, event | category | flops | bytes accessed | tf_op | source)
XLA Modules:
  0.0 166.3 jit_solution(8419400908834644309)
XLA Ops:
  0.0 164.4 %shard_map.73 = bf16[128,2560]{1,0:T(8,128)(2,1)} custom-call(s32[2,128]{1,0:T(2,128)} %bitcast.12, s32[2,128]{1,0:T(2,128)} %bitcast.13, bf16[128,2560]{1,0:T(8,128)(2,1)} %tok_ref.1, bf16[128,2560]{1,0:T(8,128)(2,1)} %fake_ref.1, bf16[864,1280]{1,0:T(8,128)(2,1)} %bitcast.9, bf16[864,1280]{1,0:T(8,128)(2,1)} %bitcast.10, bf16[864,1280]{1,0:T(8,128)(2,1)} %bitcast.11), custom_call_target="tpu_custom_call" | custom-call | flops 15288238080 | bytes 13271040 | tf_op jit(solution)/shard_map/pallas_call | solution.py:307
  164.4 2.0 %copy.9 = bf16[128,2560]{1,0:T(8,128)(2,1)} copy(bf16[128,2560]{1,0:T(8,128)(2,1)} %shard_map.73) | data formatting | bytes 1310720

commit v5 on v4

--- a/solution.py
+++ b/solution.py
@@ -16,9 +16,9 @@
 NEAR = (((1,), (1,)), ((), ()))
 
 
-def fused(ids_ref, codes_ref, tok_ref, fake_ref, wg_ref, wu_ref, wd_ref, out_ref,
+def fused(ids_ref, codes_ref, tok_ref, wg_ref, wu_ref, wd_ref, out_ref,
           near_g, near_u, far_g, far_u, down, x, sent_z, gate, up, hidden,
-          place, sib_place, sib_tok, sib_fake, combine,
+          place, sib_place, sib_tok, combine,
           part, core_in, pair_sum, y_in, y_sum, back, sib_gap, gap_in,
           far_send, far_recv, down_send, down_recv, near_sem, near_down,
           sib_send, sib_recv, z_send, z_recv, y_send, y_recv, c_send, c_recv,
@@ -59,8 +59,6 @@
     send_tok = remote(tok_ref.at[:, pl.ds(pl.multiple_of((1 - k) * half, half), half)], sib_tok,
                       sib_send.at[0], sib_recv.at[0], to_sib)
     send_tok.start()
-    send_fake = remote(fake_ref, sib_fake, sib_send.at[1], sib_recv.at[1], to_sib)
-    send_fake.start()
     own_g = pltpu.make_async_copy(wg_ref, near_g, near_sem.at[0])
     own_u = pltpu.make_async_copy(wu_ref, near_u, near_sem.at[1])
     own_g.start()
@@ -203,8 +201,6 @@
         first = (j // per_view + v) % 2 * half + (j % per_view) * wide + core * lane
         return pl.ds(pl.multiple_of(first, lane), lane)
 
-    send_fake.wait_recv()
-
     @pl.loop(0, chunks + 3)
     def _(t):
         @pl.when((t >= 1) & (t < chunks + 1))
@@ -249,9 +245,9 @@
                 return jnp.dot(combine[0, first:first + tokens], result, preferred_element_type=F32) + jnp.dot(
                     combine[1, first:first + tokens], result, preferred_element_type=F32)
 
-            sib_gap[j] = (sib_fake[:, at].astype(F32) - teacher(tokens)).astype(BF16)
+            sib_gap[j] = teacher(tokens)
             stage_d(j).start()
-            out_ref[:, at] = (fake_ref[:, at].astype(F32) - teacher(0)).astype(BF16)
+            out_ref[:, at] = teacher(0)
 
         @pl.when(t < per_view)
         def _():
@@ -286,7 +282,7 @@
 
     for j in range(per_view):
         far_down(j).wait_send()
-    for copy in (send_g, send_u, send_tok, send_fake, send_place):
+    for copy in (send_g, send_u, send_tok, send_place):
         copy.wait_send()
     for s in range(1, NE):
         z_copy(s).wait_send()
@@ -304,10 +300,10 @@
     dma = pltpu.SemaphoreType.DMA
     vmem = pl.BlockSpec(memory_space=pltpu.VMEM)
     anywhere = pl.BlockSpec(memory_space=pl.ANY)
-    return pl.pallas_call(
+    teacher = pl.pallas_call(
         fused,
-        out_shape=jax.ShapeDtypeStruct((count, D), BF16),
-        in_specs=[vmem] * 4 + [anywhere] * 3,
+        out_shape=jax.ShapeDtypeStruct((count, D), F32),
+        in_specs=[vmem] * 3 + [anywhere] * 3,
         out_specs=vmem,
         scratch_shapes=[
             pltpu.VMEM((ff, half), BF16), pltpu.VMEM((ff, half), BF16),
@@ -318,7 +314,7 @@
             pltpu.VMEM((4, total // 4, ff), F32), pltpu.VMEM((4, total // 4, ff), F32),
             pltpu.VMEM((4, total // 4, ff), BF16),
             pltpu.VMEM((2, NE * PAIR, count), BF16), pltpu.VMEM((2, NE * PAIR, count), BF16),
-            pltpu.VMEM((count, half), BF16), pltpu.VMEM((count, D), BF16),
+            pltpu.VMEM((count, half), BF16),
             pltpu.VMEM((2, 2 * count, NE * PAIR), BF16),
             pltpu.VMEM((chunks, 2, total, lane), BF16),
             pltpu.VMEM((chunks, total, lane), BF16),
@@ -326,7 +322,7 @@
             pltpu.VMEM((chunks, NE * PAIR, lane), BF16),
             pltpu.VMEM((chunks, NE, PAIR, lane), BF16),
             pltpu.VMEM((chunks, NE, PAIR, lane), BF16),
-            pltpu.VMEM((chunks, count, lane), BF16), pltpu.VMEM((chunks, count, lane), BF16),
+            pltpu.VMEM((chunks, count, lane), F32), pltpu.VMEM((chunks, count, lane), F32),
             dma((2,)), dma((2,)), dma((chunks // 2,)), dma((chunks // 2,)), dma((2,)), dma((chunks // 2,)),
             dma((3,)), dma((3,)), dma((NE - 1,)), dma((NE - 1,)), dma((NE,)), dma((NE,)),
             dma((2, NE)), dma((2, NE)),
@@ -338,9 +334,10 @@
         cost_estimate=pl.CostEstimate(
             flops=6 * total * D * ff, bytes_accessed=6 * D * ff, transcendentals=total * ff),
     )(
-        expert_ids.T, gate_codes.T, tokens, fake_score,
+        expert_ids.T, gate_codes.T, tokens,
         gate_weight[0].T, up_weight[0].T, down_weight[0],
     )
+    return (fake_score.astype(F32) - teacher).astype(BF16)
 
 
 def on_device(tokens, expert_ids, gate_codes, fake_score, gate_weight, up_weight, down_weight):

time: 167 us -> 167 us (level)
  other arithmetic: 0 us -> 2.26 us
  local copies, waits for them, and re-layouts: 1.97 us -> 0.01 us
    convert_element_type x0 -> x1, other arithmetic: none -> 2.26 us  [on_device_fused(): return (fake_score.astype(F32) - teacher).astype(BF16)]
    unnamed x1 -> x2, local copies, waits for them, and re-layouts: 1.97 us -> 0.01 us
where the time goes in v5:
time: 167 us
  Pallas kernels  165 us (99%)
  other arithmetic  2.26 us (1%)
    pallas_call x1, Pallas kernels, on_device_fused(): pl.pallas_call(fused, out_shape=jax.ShapeDtypeStruct((count, D), F32), in...  165 us

profile of v5, /device:TPU:0, one launch (start us, length us, event | category | flops | bytes accessed | tf_op | source)
XLA Modules:
  0.0 166.8 jit_solution(13416152748407826949)
XLA Ops:
  0.0 0.0 copy-start
  0.0 164.5 %shard_map.73 = f32[128,2560]{1,0:T(8,128)} custom-call(s32[2,128]{1,0:T(2,128)} %bitcast.12, s32[2,128]{1,0:T(2,128)} %bitcast.13, bf16[128,2560]{1,0:T(8,128)(2,1)} %tok_ref.1, bf16[864,1280]{1,0:T(8,128)(2,1)} %bitcast.9, bf16[864,1280]{1,0:T(8,128)(2,1)} %bitcast.10, bf16[864,1280]{1,0:T(8,128)(2,1)} %bitcast.11), custom_call_target="tpu_custom_call" | custom-call | flops 15288238080 | bytes 13271040 | tf_op jit(solution)/shard_map/pallas_call | solution.py:303
  164.5 0.0 copy-done
  164.5 2.3 %subtract_convert_fusion = bf16[128,2560]{1,0:T(8,128)(2,1)} fusion(f32[128,2560]{1,0:T(8,128)} %shard_map.73, bf16[128,2560]{1,0:T(8,128)(2,1)S(1)} %copy-done), kind=kLoop, calls=%fused_computation | loop fusion | flops 983040 | bytes 2621440 | tf_op jit(solution)/shard_map/convert_element_type | solution.py:340
Async XLA Ops:
  0.0 164.5 %copy-start = (bf16[128,2560]{1,0:T(8,128)(2,1)S(1)}, bf16[128,2560]{1,0:T(8,128)(2,1)}, u32[]{:S(2)}) copy-start(bf16[128,2560]{1,0:T(8,128)(2,1)} %param.10) | copy-start | bytes 1966084
